TPU v7x, 256 devices: a whole 4x4x8 slice. The times are simulated.
256 devices in a mesh: dp: 16 (over z, core), tp: 16 (over y, x).
Axes of the slice: x: 4, y: 4, z: 8, core: 2. Of those that a mesh axis runs over, the one named last changes fastest.
Arguments:
- queries: bfloat16 [256, 128, 576], P(('dp', 'tp')), may hold values from -14 to 14
- new_latent: bfloat16 [256, 576], P(('dp', 'tp')), may hold values from -6 to 6
- latent_cache: bfloat16 [256, 1024, 576], P(('dp', 'tp')), may hold values from -6 to 6
- cached_lengths: int32 [256], P(('dp', 'tp')), may hold values from 1 to 1024, as said below
- value_up: bfloat16 [128, 512, 128], P('tp'), may hold values from -0.25 to 0.25
- out_weight: bfloat16 [16384, 7168], P('tp', 'dp'), may hold values from -0.046875 to 0.046875
- residual_in: bfloat16 [256, 7168], P('tp', 'dp'), may hold values from -0.3125 to 0.3125
- norm_gain: float32 [7168], P('dp'), may hold values from 0.5 to 1.5
- gate_weight: bfloat16 [7168, 18432], P('dp', 'tp'), may hold values from -0.0625 to 0.0625
- up_weight: bfloat16 [7168, 18432], P('dp', 'tp'), may hold values from -0.0625 to 0.0625
- down_weight: bfloat16 [18432, 7168], P('tp', 'dp'), may hold values from -0.046875 to 0.046875
Outputs:
- layer_out: bfloat16 [256, 7168], P('tp', 'dp')
Inputs may be any that keep to these rules, and one draw needn't show every extreme that they name: `cached_lengths`: cached positions of each request; some request has all 1024.
All inputs are finite; a program needn't handle non-finite values.
Results may differ from a plain program's by a relative error of at most 0.02.
Values may be sent and summed in bfloat16 or wider, within the bound.
A program may use at most 64 MiB of HBM per device.

v0:
```python
import jax
import jax.numpy as jnp
from jax import lax
from jax.sharding import PartitionSpec as P

D = 7168
LATENT = 512
ROPE = 64
NOPE = 128


def attend(queries, new_latent, latent_cache, cached_lengths, block_count, block_rows):
    score_scale = (NOPE + ROPE) ** (-0.5)
    own_score = (
        jnp.einsum("rhc,rc->rh", queries, new_latent, preferred_element_type=jnp.float32)
        * score_scale
    )
    start_total = jnp.ones_like(own_score)
    start_accum = jnp.broadcast_to(
        new_latent[:, None, :LATENT].astype(jnp.float32),
        (queries.shape[0], queries.shape[1], LATENT),
    )

    def visit(block_index, running):
        top_score, total_weight, accum = running
        key_block = lax.dynamic_slice_in_dim(latent_cache, block_index * block_rows, block_rows, 1)
        scores = (
            jnp.einsum("rhc,rkc->rhk", queries, key_block, preferred_element_type=jnp.float32)
            * score_scale
        )
        position = block_index * block_rows + jnp.arange(block_rows)
        scores = jnp.where(position[None, None, :] < cached_lengths[:, None, None], scores, -1e30)
        new_top = jnp.maximum(top_score, jnp.max(scores, axis=2))
        rescale = jnp.exp(top_score - new_top)
        weights = jnp.exp(scores - new_top[:, :, None])
        total_weight = total_weight * rescale + jnp.sum(weights, axis=2)
        rounded = weights.astype(jnp.bfloat16)
        added = jnp.einsum(
            "rhk,rkc->rhc", rounded, key_block[:, :, :LATENT], preferred_element_type=jnp.float32
        )
        accum = accum * rescale[:, :, None] + added
        return (new_top, total_weight, accum)

    top_score, total_weight, accum = lax.fori_loop(
        0, block_count, visit, (own_score, start_total, start_accum)
    )
    return (accum / total_weight[:, :, None]).astype(jnp.bfloat16)


def shards(
    queries,
    new_latent,
    latent_cache,
    cached_lengths,
    value_up,
    out_weight,
    residual_in,
    norm_gain,
    gate_weight,
    up_weight,
    down_weight,
):
    block_rows = min(512, latent_cache.shape[1])
    block_count = latent_cache.shape[1] // block_rows
    head_latent = attend(queries, new_latent, latent_cache, cached_lengths, block_count, block_rows)
    owned_heads = lax.all_to_all(head_latent, "tp", split_axis=1, concat_axis=0, tiled=True)
    values = jnp.einsum("rhc,hcv->rhv", owned_heads, value_up, preferred_element_type=jnp.float32)
    values = values.astype(jnp.bfloat16).reshape(owned_heads.shape[0], -1)
    all_values = lax.all_gather(values, "dp", axis=0, tiled=True)
    row_block = all_values
    attention_out = lax.psum_scatter(
        jnp.dot(row_block, out_weight, preferred_element_type=jnp.float32),
        "tp",
        scatter_dimension=0,
        tiled=True,
    )
    stream = residual_in.astype(jnp.float32) + attention_out
    partial_value = jnp.sum(stream * stream, axis=1)
    square_sum = lax.psum(partial_value, "dp")
    normed = (stream * lax.rsqrt(square_sum / D + 1e-06)[:, None] * norm_gain[None, :]).astype(
        jnp.bfloat16
    )
    row_piece = lax.all_gather(normed, "tp", axis=0, tiled=True)
    gate_part = jnp.dot(row_piece, gate_weight, preferred_element_type=jnp.float32)
    up_part = jnp.dot(row_piece, up_weight, preferred_element_type=jnp.float32)
    gate_up = jnp.concatenate([gate_part, up_part], axis=1)
    unit_width = gate_weight.shape[1]
    gate_sum = gate_up[:, :unit_width]
    up_sum = gate_up[:, unit_width:]
    gate_sum, up_sum = lax.psum((gate_sum, up_sum), "dp")
    hidden = (jax.nn.silu(gate_sum) * up_sum).astype(jnp.bfloat16)
    row_block = hidden
    lowered = lax.psum_scatter(
        jnp.dot(row_block, down_weight, preferred_element_type=jnp.float32).astype(jnp.bfloat16),
        "tp",
        scatter_dimension=0,
        tiled=True,
    ).astype(jnp.float32)
    return (stream + lowered).astype(jnp.bfloat16)


def solution(mesh):
    in_specs = (
        P(("dp", "tp"), None, None),
        P(("dp", "tp"), None),
        P(("dp", "tp"), None, None),
        P(("dp", "tp")),
        P("tp", None, None),
        P("tp", "dp"),
        P("tp", "dp"),
        P("dp"),
        P("dp", "tp"),
        P("dp", "tp"),
        P("tp", "dp"),
    )
    out_specs = P("tp", "dp")
    return jax.shard_map(shards, mesh=mesh, in_specs=in_specs, out_specs=out_specs, check_vma=False)
```

profile of v0, /device:TPU:16, one launch (start us, length us, event | category | flops | bytes accessed | tf_op | source)
XLA Modules:
  0.0 383.0 jit_solution(8920998323993219236)
XLA Ops:
  6.5 0.0 copy-start
  6.5 0.0 reduce-scatter.3.cloned.1.call-start
  6.5 0.8 slice_convert_fusion
  7.3 1.0 fusion.16
  8.4 7.4 %while.18 = (s32[]{:T(128)}, f32[1,128]{1,0:T(1,128)S(1)}, f32[1,128]{1,0:T(1,128)S(1)}, f32[1,128,512]{2,1,0:T(8,128)S(1)}, s32[1]{0:T(128)}, /*index=5*/bf16[1...) while((s32[]{:T(128)}, f32[1,128]{1,0:T(1,128)S(1)}, ...), condition=%wide.region_3.4_spmd.clone, body=%wide.region_0.3_spmd.clone.sunk | while | flops 143197696 | bytes 2581693 | solution.py:44
  8.4 0.7 add_compare_fusion.2
  9.1 1.5 fusion.40
  10.6 0.1 fusion.42
  10.7 1.4 fusion.44
  12.1 0.7 add_compare_fusion.2
  12.8 1.5 fusion.40
  14.3 0.1 fusion.42
  14.4 1.4 fusion.44
  15.8 0.1 divide_convert_fusion
  15.9 0.2 copy.30
  16.1 0.5 broadcast.70
  16.6 1.4 reduce.10
  18.0 0.1 reshape.97
  18.1 12.6 %all_to_all.12 = bf16[16,2,2048]{2,1,0:T(2,128)(2,1)S(1)} all-to-all(bf16[16,2,2048]{2,1,0:T(2,128)(2,1)S(1)} %reshape.97), channel_id=1, replica_groups=mesh['dp'=16,'tp'=16] {'tp'}, dimensions={0} | all-to-all | bytes 262144 | tf_op jit(solution)/shard_map/all_to_all | solution.py:66
  30.7 0.1 reshape.98
  30.8 0.0 copy-start.3
  30.9 0.0 copy-done
  30.9 0.3 fusion.14
  31.2 21.4 %all_gather.6 = bf16[256,1024]{1,0:T(8,128)(2,1)S(1)} all-gather(bf16[16,1024]{1,0:T(8,128)(2,1)S(1)} %bitcast.84), channel_id=1, replica_groups=mesh['dp'=16,'tp'=16] {'dp'}, dimensions={0}, use_global_device_ids=true | all-gather | bytes 557056 | tf_op jit(solution)/shard_map/all_gather | solution.py:69
  52.6 0.0 copy-done.3
  52.6 0.0 copy-start.5
  52.6 0.0 copy-start.6
  52.6 0.0 copy-start.1
  52.6 1.3 fusion.22
  53.8 0.0 reduce-scatter.3.cloned.1.call-update
  53.9 0.0 all-reduce.3.cloned.1.call-start
  53.9 73.5 %reduce-scatter.3.cloned.1.call-done = f32[16,448]{1,0:T(8,128)} async-done(((f32[256,448]{1,0:T(8,128)}), f32[16,448]{1,0:T(8,128)}) %reduce-scatter.3.cloned.1.call-update) | async-done | bytes 28688 | tf_op jit(solution)/shard_map/reduce_scatter | solution.py:71
  127.4 0.0 copy-done.5
  127.4 0.9 multiply_reduce_fusion
  128.3 24.1 %psum.21 = f32[16]{0:T(128)S(1)} all-reduce(f32[16]{0:T(128)S(1)} %multiply_reduce_fusion), channel_id=1, replica_groups=mesh['dp'=16,'tp'=16] {'dp'}, use_global_device_ids=true, to_apply=%region_6.7 | all-reduce | flops 16 | bytes 128 | tf_op jit(solution)/shard_map/psum | solution.py:79
  152.4 0.0 copy-done.6
  152.4 0.8 multiply_convert_fusion.2
  153.2 22.4 %all_gather.7 = bf16[256,448]{1,0:T(8,128)(2,1)S(1)} all-gather(bf16[16,448]{1,0:T(8,128)(2,1)S(1)} %multiply_convert_fusion.2), channel_id=1, replica_groups=mesh['dp'=16,'tp'=16] {'tp'}, dimensions={0}, use_global_device_ids=true | all-gather | bytes 243712 | tf_op jit(solution)/shard_map/all_gather | solution.py:83
  175.6 0.0 copy-done.1
  175.6 0.0 copy-start.2
  175.7 1.5 fusion.24
  177.2 0.0 copy-done.2
  177.2 1.5 fusion.23
  178.7 0.0 copy-start.7
  178.7 0.0 all-reduce.3.cloned.1.call-update
  178.7 0.0 reduce-scatter.5.cloned.1.call-start
  178.8 115.8 %all-reduce.3.cloned.1.call-done = (f32[256,1152]{1,0:T(8,128)}, f32[256,1152]{1,0:T(8,128)}) async-done(((f32[256,1152]{1,0:T(8,128)}, f32[256,1152]{1,0:T(8,128)}), (f32[256,1152]{1,0:T(8,128)}, f32[256,1152]{1,0:T(8,128)})) %all-reduce.3.cloned.1.call-update) | async-done | bytes 2359312 | tf_op jit(solution)/shard_map/psum | solution.py:90
  294.5 0.0 copy-done.7
  294.5 0.0 copy-start.4
  294.5 2.9 convolution_convert_fusion
  297.4 0.0 reduce-scatter.5.cloned.1.call-update
  297.5 77.7 %reduce-scatter.5.cloned.1.call-done = bf16[16,448]{1,0:T(8,128)(2,1)} async-done(((bf16[256,448]{1,0:T(8,128)(2,1)}), bf16[16,448]{1,0:T(8,128)(2,1)}) %reduce-scatter.5.cloned.1.call-update) | async-done | bytes 14352 | tf_op jit(solution)/shard_map/reduce_scatter | solution.py:93
  375.2 0.0 copy-done.4
  375.2 1.3 add_convert_fusion
  (11 shorter events, 0.1 us)
Async XLA Ops:
  6.5 24.3 %copy-start = (bf16[8,512,128]{2,1,0:T(8,128)(2,1)S(1)}, bf16[8,512,128]{2,1,0:T(8,128)(2,1)}, u32[]{:S(2)}) copy-start(bf16[8,512,128]{2,1,0:T(8,128)(2,1)} %param.17) | copy-start | bytes 3145732
  6.5 120.9 %reduce-scatter.3.cloned.1.call-start = ((), (), s32[]{:S(2)}) async-start(), calls=%async_computation.3 | async-start | bytes 557056 | tf_op jit(solution)/shard_map/reduce_scatter | solution.py:71
  30.8 21.8 %copy-start.3 = (bf16[1024,448]{0,1:T(8,128)(2,1)S(1)}, bf16[1024,448]{0,1:T(8,128)(2,1)}, u32[]{:S(2)}) copy-start(bf16[1024,448]{0,1:T(8,128)(2,1)} %param.18) | copy-start | bytes 2752516
  52.6 74.8 %copy-start.5 = (bf16[16,448]{1,0:T(8,128)(2,1)S(1)}, bf16[16,448]{1,0:T(8,128)(2,1)}, u32[]{:S(2)}) copy-start(bf16[16,448]{1,0:T(8,128)(2,1)} %param.19) | copy-start | bytes 43012
  52.6 99.8 %copy-start.6 = (f32[448]{0:T(512)S(1)}, f32[448]{0:T(512)}, u32[]{:S(2)}) copy-start(f32[448]{0:T(512)} %param.20) | copy-start | bytes 5380
  52.6 123.1 %copy-start.1 = (bf16[448,1152]{1,0:T(8,128)(2,1)S(1)}, bf16[448,1152]{1,0:T(8,128)(2,1)}, u32[]{:S(2)}) copy-start(bf16[448,1152]{1,0:T(8,128)(2,1)} %param.22) | copy-start | bytes 3096580
  53.9 240.7 %all-reduce.3.cloned.1.call-start = ((), (), s32[]{:S(2)}) async-start(), calls=%async_computation.5 | async-start | bytes 4718592 | tf_op jit(solution)/shard_map/psum | solution.py:90
  175.6 1.5 copy-start.2
  178.7 115.9 %copy-start.7 = (bf16[1152,448]{0,1:T(8,128)(2,1)S(1)}, bf16[1152,448]{0,1:T(8,128)(2,1)}, u32[]{:S(2)}) copy-start(bf16[1152,448]{0,1:T(8,128)(2,1)} %param.23) | copy-start | bytes 3096580
  178.7 196.5 %reduce-scatter.5.cloned.1.call-start = ((), (), s32[]{:S(2)}) async-start(), calls=%async_computation.4 | async-start | bytes 278528 | tf_op jit(solution)/shard_map/reduce_scatter | solution.py:93
  294.5 80.6 %copy-start.4 = (f32[16,448]{1,0:T(8,128)S(1)}, f32[16,448]{1,0:T(8,128)}, u32[]{:S(2)}) copy-start(f32[16,448]{1,0:T(8,128)} %reduce-scatter.3.cloned.1.call-done) | copy-start | bytes 86020
Sparse Core Ops, SparseCore 0:
  54.0 73.3 reduce-scatter.2
  178.8 115.6 all-reduce.2
  298.4 76.7 reduce-scatter.4
where the time goes:
time: 384 us; the launch traced here: 383 us
  waiting for transfers between devices  267 us (70%)
  blocking collectives  80.5 us (21%)
  matrix products  14.2 us (4%)
  between operations  13.2 us (3%)
  other arithmetic  6.86 us (2%)
    psum x1, waiting for transfers between devices, shards(): gate_sum, up_sum = lax.psum((gate_sum, up_sum), 'dp')  116 us
    reduce_scatter x1, waiting for transfers between devices, shards(): lax.psum_scatter(jnp.dot(row_block, down_weight, preferred_element_type=j...  77.7 us
    reduce_scatter x1, waiting for transfers between devices, shards(): lax.psum_scatter(jnp.dot(row_block, out_weight, preferred_element_type=jn...  73.5 us
    psum x1, blocking collectives, shards(): square_sum = lax.psum(partial_value, 'dp')  24.1 us
    all_gather x1, blocking collectives, shards(): row_piece = lax.all_gather(normed, 'tp', axis=0, tiled=True)  22.4 us
    all_gather x1, blocking collectives, shards(): all_values = lax.all_gather(values, 'dp', axis=0, tiled=True)  21.4 us
    all_to_all x1, blocking collectives, shards(): lax.all_to_all(head_latent, 'tp', split_axis=1, concat_axis=0, tiled=True)  12.6 us
  transfers between devices with their start and end apart: 3, of which 3 were waited for; matrix products, arithmetic and copies ran while one was open for 0% of the time, Pallas kernels for 0%

commit v1 on v0

v1 whole, which is shorter than its diff:
```python
import jax
import jax.numpy as jnp
from jax import lax
from jax.experimental import pallas as pl
from jax.experimental.pallas import tpu as pltpu
from jax.sharding import PartitionSpec as P

D = 7168
HEADS = 128
LATENT = 512
KEY = 576
CACHE = 1024
SCALE = (128 + 64) ** (-0.5)
PLANE = 16
CHIPS = 8
ROWS = 16
OWN_HEADS = 8
VALUES = 1024
FEAT = 448
PAD = 512
UNITS = 1152
WIDE = 2 * UNITS + 128
F32 = jnp.float32
BF16 = jnp.bfloat16
MESH = pl.DeviceIdType.MESH


def kernel(
    queries,
    fresh,
    cache,
    length,
    value_up,
    out_weight,
    residual,
    gain,
    gate_weight,
    up_weight,
    down_weight,
    out,
    q_v,
    k_v,
    vu_v,
    ow_v,
    gu_v,
    dw_v,
    head_out,
    head_in,
    val,
    o_out,
    o_in,
    x_out,
    x_in,
    part,
    ring_l,
    ring_s,
    got_l,
    got_s,
    hid,
    d_out,
    d_in,
    load_sem,
    swap_send,
    swap_recv,
    head_send,
    head_recv,
    val_send,
    val_recv,
    o_send,
    o_recv,
    x_send,
    x_recv,
    ring_send,
    ring_recv,
    hid_send,
    hid_recv,
    d_send,
    d_recv,
):
    dp, tp = lax.axis_index("dp"), lax.axis_index("tp")
    z, core = lax.div(dp, 2), lax.rem(dp, 2)
    way = 1 - 2 * core
    tp_chip, tp_core = lax.div(tp, 2), lax.rem(tp, 2)
    sibling = (dp + way, tp)

    def chip(steps):
        return lax.rem(z + way * steps + CHIPS, CHIPS)

    ahead = (2 * chip(1) + core, tp)
    behind = (2 * chip(-1) + core, tp)

    def column(steps):
        return lax.rem(tp + steps, PLANE)

    sent = []

    def push(src, dst, send_sem, recv_sem, device):
        copy = pltpu.make_async_remote_copy(src, dst, send_sem, recv_sem, device, MESH)
        copy.start()
        sent.append(copy)
        return copy

    def finish():
        for copy in sent:
            copy.wait_send()

    def load(src, dst, i):
        copy = pltpu.make_async_copy(src, dst, load_sem.at[i])
        copy.start()
        return copy

    gu_v[FEAT:PAD, :] = jnp.zeros((PAD - FEAT, WIDE), BF16)
    gu_v[PAD + FEAT :, :] = jnp.zeros((PAD - FEAT, WIDE), BF16)
    gu_v[:, 2 * UNITS :] = jnp.zeros((2 * PAD, WIDE - 2 * UNITS), BF16)
    row = lax.broadcasted_iota(jnp.int32, (16, 128), 0)
    ones = jnp.where(row < 2, 1.0, 0.0).astype(BF16)
    gu_v[FEAT : FEAT + 16, 2 * UNITS :] = ones
    gu_v[PAD + FEAT : PAD + FEAT + 16, 2 * UNITS :] = ones

    load_q = load(queries.at[0], q_v, 0)
    load_k = load(cache.at[0], k_v, 1)

    barrier = pltpu.get_barrier_semaphore()
    for i in range(1, PLANE):
        pl.semaphore_signal(barrier, inc=1, device_id=(dp, column(i)), device_id_type=MESH)
    for i in range(PLANE):
        pl.semaphore_signal(
            barrier, inc=1, device_id=(dp + way, column(i)), device_id_type=MESH
        )
    for device in (ahead, behind):
        pl.semaphore_signal(barrier, inc=1, device_id=device, device_id_type=MESH)

    load_vu = [
        load(value_up.at[h], vu_v.at[:, pl.ds(128 * h, 128)], 2 + h) for h in range(OWN_HEADS)
    ]
    mine = pl.ds(pl.multiple_of(core * PAD, PAD), FEAT)
    weights = [
        (out_weight, ow_v.at[core]),
        (gate_weight, gu_v.at[mine, pl.ds(0, UNITS)]),
        (up_weight, gu_v.at[mine, pl.ds(UNITS, UNITS)]),
        (down_weight, dw_v.at[core]),
    ]
    load_w = [load(src, dst, 10 + i) for i, (src, dst) in enumerate(weights)]

    load_q.wait()
    load_k.wait()
    q = q_v[...]
    scores = lax.dot_general(
        q, k_v[...], (((1,), (1,)), ((), ())), preferred_element_type=F32
    )
    pl.semaphore_wait(barrier, 2 * PLANE + 1)
    swaps = [
        push(src, dst, swap_send.at[i], swap_recv.at[i], sibling)
        for i, (src, dst) in enumerate(weights)
    ]
    position = lax.broadcasted_iota(jnp.int32, (HEADS, CACHE), 1)
    scores = jnp.where(position < length[0], scores * SCALE, -1e30)
    new = fresh[...].astype(F32)
    own = jnp.sum(q.astype(F32) * new, axis=1, keepdims=True) * SCALE
    top = jnp.maximum(own, jnp.max(scores, axis=1, keepdims=True))
    weight = jnp.exp(scores - top)
    own_weight = jnp.exp(own - top)
    total = jnp.sum(weight, axis=1, keepdims=True) + own_weight
    summed = jnp.dot(weight.astype(BF16), k_v[:, :LATENT], preferred_element_type=F32)
    latent = ((summed + own_weight * new[:, :LATENT]) / total).reshape(PLANE, OWN_HEADS, LATENT)
    half = LATENT // 2
    head_out[...] = jnp.concatenate([latent[:, :, :half], latent[:, :, half:]], axis=1).astype(BF16)

    for i in range(1, PLANE):
        push(
            head_out.at[column(i)],
            head_in.at[tp],
            head_send.at[i],
            head_recv.at[i],
            (dp, column(i)),
        )
    head_in[tp] = head_out[tp]
    for copy in load_vu:
        copy.wait()
    for i in range(1, PLANE):
        slot = head_in.at[column(PLANE - i)]
        pltpu.make_async_remote_copy(
            slot, slot, head_send.at[i], head_recv.at[i], (dp, tp), MESH
        ).wait_recv()


    wide = head_in[...].astype(F32)
    latents = jnp.concatenate([wide[:, :OWN_HEADS], wide[:, OWN_HEADS:]], axis=2)
    latents = latents.reshape(PLANE * OWN_HEADS, LATENT).astype(BF16)
    products = jnp.dot(latents, vu_v[...], preferred_element_type=F32)
    row_head = lax.broadcasted_iota(jnp.int32, products.shape, 0) & (OWN_HEADS - 1)
    column_head = lax.broadcasted_iota(jnp.int32, products.shape, 1) >> 7
    products = jnp.where(row_head == column_head, products, 0.0).astype(BF16)
    to_row = lax.broadcasted_iota(jnp.int32, (ROWS, PLANE * OWN_HEADS), 0)
    from_row = lax.broadcasted_iota(jnp.int32, (ROWS, PLANE * OWN_HEADS), 1) >> 3
    pick = jnp.where(to_row == from_row, 1.0, 0.0).astype(BF16)
    val[z] = jnp.dot(pick, products, preferred_element_type=F32).astype(BF16)

    def gather(buf, send_sem, recv_sem, use):
        def step(slot, i, device):
            return push(buf.at[slot], buf.at[slot], send_sem.at[i], recv_sem.at[i], device)

        def arrived(slot, i):
            ref = buf.at[slot]
            pltpu.make_async_remote_copy(
                ref, ref, send_sem.at[i], recv_sem.at[i], ahead, MESH
            ).wait_recv()

        step(z, 0, ahead)
        step(z, 4, behind)
        use([z], 0)
        for j in range(1, 5):
            arrived(chip(-j), j - 1)
            if j < 4:
                step(chip(-j), j, ahead)
                arrived(chip(j), 3 + j)
                if j < 3:
                    step(chip(j), 4 + j, behind)
            use([chip(-j), chip(j)] if j < 4 else [chip(-j)], 2 * j - 1)

    def project(buf, w, dst_out, dst_in, send_sem, recv_sem):
        def use(chips, first):
            rows = jnp.concatenate([buf[c] for c in chips], axis=0) if len(chips) > 1 else buf[chips[0]]
            for to in range(2):
                sums = jnp.dot(rows, w[to], preferred_element_type=F32).astype(BF16)
                for n, c in enumerate(chips):
                    dst_out[c, to, :, :FEAT] = sums[n * ROWS : (n + 1) * ROWS]
            for n, c in enumerate(chips):
                owner = 2 * c + core
                i = first + n
                push(
                    dst_out.at[c, 1 - core],
                    dst_in.at[tp],
                    send_sem.at[i, 0],
                    recv_sem.at[tp],
                    (dp + way, owner),
                )

                @pl.when(owner != tp)
                def _():
                    pltpu.make_async_remote_copy(
                        dst_out.at[c, core],
                        dst_in.at[tp],
                        send_sem.at[i, 1],
                        recv_sem.at[tp],
                        (dp, owner),
                        MESH,
                    ).start()

                @pl.when(owner == tp)
                def _():
                    dst_in[tp] = dst_out[c, core]

        return use

    def project_sent(dst_out, send_sem):
        for i in range(CHIPS):
            c = z if i == 0 else chip(-((i + 1) // 2)) if i % 2 else chip(i // 2)

            @pl.when(2 * c + core != tp)
            def _():
                ref = dst_out.at[c, core]
                pltpu.make_async_remote_copy(
                    ref, ref, send_sem.at[i, 1], send_sem.at[i, 1], ahead, MESH
                ).wait_send()

    def collect(dst_in, recv_sem):
        for i in range(PLANE):
            src = column(i)

            def arrived():
                ref = dst_in.at[src]
                pltpu.make_async_remote_copy(
                    ref, ref, recv_sem.at[src], recv_sem.at[src], ahead, MESH
                ).wait_recv()

            if i == 0:
                pl.when(core != tp_core)(arrived)
            else:
                arrived()
        return jnp.sum(dst_in[...].astype(F32), axis=0)

    load_w[0].wait()
    swaps[0].wait_recv()
    gather(val, val_send, val_recv, project(val, ow_v, o_out, o_in, o_send, o_recv))
    attention = collect(o_in, o_recv)
    stream = residual[...].astype(F32) + attention[:, :FEAT]

    squares = jnp.sum(stream * stream, axis=1, keepdims=True)
    high = squares.astype(BF16).astype(F32)
    lane = lax.broadcasted_iota(jnp.int32, (ROWS, PAD - FEAT), 1)
    extra = jnp.where(lane == 0, high, jnp.where(lane == 1, squares - high, 0.0))
    x_out[:, :FEAT] = (stream * gain[...]).astype(BF16)
    x_out[:, FEAT:] = extra.astype(BF16)
    x_slot = x_in.at[tp_chip, core]
    for i in range(1, PLANE):
        push(
            x_out,
            x_slot,
            x_send.at[i],
            x_recv.at[tp_chip, core],
            (2 * z + tp_core, column(i)),
        )

    def x_to_sibling():
        return pltpu.make_async_remote_copy(
            x_out, x_slot, x_send.at[0], x_recv.at[tp_chip, core], sibling, MESH
        )

    @pl.when(tp_core != core)
    def _():
        x_to_sibling().start()

    @pl.when(tp_core == core)
    def _():
        x_in[tp_chip, core] = x_out[...]

    def x_wait(c):
        for src in range(2):

            @pl.when(jnp.logical_or(2 * c + core != tp, core != src))
            def _():
                ref = x_in.at[c, src]
                pltpu.make_async_remote_copy(
                    ref, ref, x_recv.at[c, src], x_recv.at[c, src], ahead, MESH
                ).wait_recv()

    def gate_up(i):
        to_l, to_s = chip(4 - i), chip(i - 3)
        x_wait(to_l)
        x_wait(to_s)
        rows = jnp.concatenate(
            [
                jnp.concatenate([x_in[to_l, 0], x_in[to_l, 1]], axis=1),
                jnp.concatenate([x_in[to_s, 0], x_in[to_s, 1]], axis=1),
            ],
            axis=0,
        )
        part[i] = jnp.dot(rows, gu_v[...], preferred_element_type=F32)

    cuts = [(0, 1280), (1280, 1152)]

    def ring(out_buf, in_buf, i, n, side, device):
        lo, size = cuts[n]
        mine = part[i, side * ROWS : (side + 1) * ROWS, lo : lo + size]
        if i > 0:
            ref = in_buf.at[i - 1, :, pl.ds(lo, size)]
            pltpu.make_async_remote_copy(
                ref, ref, ring_send.at[side, i - 1, n], ring_recv.at[side, i - 1, n], ahead, MESH
            ).wait_recv()
            mine = mine + in_buf[i - 1, :, lo : lo + size].astype(F32)
        out_buf[i, :, lo : lo + size] = mine.astype(BF16)
        push(
            out_buf.at[i, :, pl.ds(lo, size)],
            in_buf.at[i, :, pl.ds(lo, size)],
            ring_send.at[side, i, n],
            ring_recv.at[side, i, n],
            device,
        )

    for copy in load_w[1:3]:
        copy.wait()
    for copy in swaps[1:3]:
        copy.wait_recv()
    for i in range(4):
        gate_up(i)
        for n in range(len(cuts)):
            ring(ring_l, got_l, i, n, 0, ahead)
            if i < 3:
                ring(ring_s, got_s, i, n, 1, behind)
    whole = []
    for n, (lo, size) in enumerate(cuts):
        mine = part[3, ROWS:, lo : lo + size]
        for side, i, buf in ((1, 2, got_s), (0, 3, got_l)):
            ref = buf.at[i, :, pl.ds(lo, size)]
            pltpu.make_async_remote_copy(
                ref, ref, ring_send.at[side, i, n], ring_recv.at[side, i, n], ahead, MESH
            ).wait_recv()
            mine = mine + buf[i, :, lo : lo + size].astype(F32)
        whole.append(mine)
    whole = jnp.concatenate(whole, axis=1)
    inverse = lax.rsqrt(whole[:, 2 * UNITS : 2 * UNITS + 1] * (1.0 / D) + 1e-06)
    gate = whole[:, :UNITS] * inverse
    up = whole[:, UNITS : 2 * UNITS] * inverse
    hid[z] = (gate / (1.0 + jnp.exp(-gate)) * up).astype(BF16)

    load_w[3].wait()
    swaps[3].wait_recv()
    gather(hid, hid_send, hid_recv, project(hid, dw_v, d_out, d_in, d_send, d_recv))
    lowered = collect(d_in, d_recv)
    out[...] = (stream + lowered[:, :FEAT]).astype(BF16)

    finish()
    project_sent(o_out, o_send)
    project_sent(d_out, d_send)

    @pl.when(tp_core != core)
    def _():
        x_to_sibling().wait_send()


def layer(
    queries,
    new_latent,
    latent_cache,
    cached_lengths,
    value_up,
    out_weight,
    residual_in,
    norm_gain,
    gate_weight,
    up_weight,
    down_weight,
):
    anywhere = pl.BlockSpec(memory_space=pl.ANY)
    vmem = pl.BlockSpec(memory_space=pltpu.VMEM)
    smem = pl.BlockSpec(memory_space=pltpu.SMEM)
    dma = pltpu.SemaphoreType.DMA
    return pl.pallas_call(
        kernel,
        out_shape=jax.ShapeDtypeStruct((ROWS, FEAT), BF16),
        in_specs=[
            anywhere,
            vmem,
            anywhere,
            smem,
            anywhere,
            anywhere,
            vmem,
            vmem,
            anywhere,
            anywhere,
            anywhere,
        ],
        out_specs=vmem,
        scratch_shapes=[
            pltpu.VMEM((HEADS, KEY), BF16),
            pltpu.VMEM((CACHE, KEY), BF16),
            pltpu.VMEM((LATENT, VALUES), BF16),
            pltpu.VMEM((2, VALUES, FEAT), BF16),
            pltpu.VMEM((2 * PAD, WIDE), BF16),
            pltpu.VMEM((2, UNITS, FEAT), BF16),
            pltpu.VMEM((PLANE, ROWS, LATENT // 2), BF16),
            pltpu.VMEM((PLANE, ROWS, LATENT // 2), BF16),
            pltpu.VMEM((CHIPS, ROWS, VALUES), BF16),
            pltpu.VMEM((CHIPS, 2, ROWS, PAD), BF16),
            pltpu.VMEM((PLANE, ROWS, PAD), BF16),
            pltpu.VMEM((ROWS, PAD), BF16),
            pltpu.VMEM((CHIPS, 2, ROWS, PAD), BF16),
            pltpu.VMEM((4, 2 * ROWS, WIDE), F32),
            pltpu.VMEM((4, ROWS, WIDE), BF16),
            pltpu.VMEM((3, ROWS, WIDE), BF16),
            pltpu.VMEM((4, ROWS, WIDE), BF16),
            pltpu.VMEM((3, ROWS, WIDE), BF16),
            pltpu.VMEM((CHIPS, ROWS, UNITS), BF16),
            pltpu.VMEM((CHIPS, 2, ROWS, PAD), BF16),
            pltpu.VMEM((PLANE, ROWS, PAD), BF16),
            dma((14,)),
            dma((4,)),
            dma((4,)),
            dma((PLANE,)),
            dma((PLANE,)),
            dma((7,)),
            dma((7,)),
            dma((CHIPS, 2)),
            dma((PLANE,)),
            dma((PLANE,)),
            dma((CHIPS, 2)),
            dma((2, 4, 2)),
            dma((2, 4, 2)),
            dma((7,)),
            dma((7,)),
            dma((CHIPS, 2)),
            dma((PLANE,)),
        ],
        compiler_params=pltpu.CompilerParams(
            collective_id=0, has_side_effects=True, vmem_limit_bytes=48 * 1024 * 1024
        ),
    )(
        queries,
        new_latent,
        latent_cache,
        cached_lengths,
        value_up,
        out_weight,
        residual_in,
        norm_gain.reshape(1, FEAT),
        gate_weight,
        up_weight,
        down_weight,
    )


def solution(mesh):
    in_specs = (
        P(("dp", "tp"), None, None),
        P(("dp", "tp"), None),
        P(("dp", "tp"), None, None),
        P(("dp", "tp")),
        P("tp", None, None),
        P("tp", "dp"),
        P("tp", "dp"),
        P("dp"),
        P("dp", "tp"),
        P("dp", "tp"),
        P("tp", "dp"),
    )
    return jax.shard_map(
        layer, mesh=mesh, in_specs=in_specs, out_specs=P("tp", "dp"), check_vma=False
    )
```

time: 384 us -> 84.1 us (0.22)
  waiting for transfers between devices: 267 us -> 0 us
  blocking collectives: 80.5 us -> 0 us
  Pallas kernels: 0 us -> 74.1 us
  matrix products: 14.2 us -> 0 us
  between operations: 13.2 us -> 0.83 us
  local copies, waits for them, and re-layouts: 0.99 us -> 8.89 us
  other arithmetic: 6.86 us -> 0 us
    reduce_scatter x2 -> x0, waiting for transfers between devices: 151 us -> none  [the longest x1 77.7 us: shards(): lax.psum_scatter(jnp.dot(row_block, down_weight, preferred_element_type=j...]
    psum x1 -> x0, waiting for transfers between devices: 116 us -> none  [shards(): gate_sum, up_sum = lax.psum((gate_sum, up_sum), 'dp')]
    pallas_call x0 -> x1, Pallas kernels: none -> 74.1 us  [layer(): pl.pallas_call(kernel, out_shape=jax.ShapeDtypeStruct((ROWS, FEAT), BF16)...]
    all_gather x2 -> x0, blocking collectives: 43.8 us -> none  [the longest x1 22.4 us: shards(): row_piece = lax.all_gather(normed, 'tp', axis=0, tiled=True)]
    psum x1 -> x0, blocking collectives: 24.1 us -> none  [shards(): square_sum = lax.psum(partial_value, 'dp')]
    dot_general x10 -> x0, matrix products: 14.2 us -> none  [the longest x2 2.96 us: visit(): jnp.einsum('rhc,rkc->rhk', queries, key_block, preferred_element_type=jnp...]
    all_to_all x1 -> x0, blocking collectives: 12.6 us -> none  [shards(): lax.all_to_all(head_latent, 'tp', split_axis=1, concat_axis=0, tiled=True)]
    unnamed x20 -> x19, local copies, waits for them, and re-layouts: 0.75 us -> 8.89 us
  transfers between devices with their start and end apart: 3 -> 0, of which waited for: 3 -> 0; matrix products, arithmetic and copies ran while one was open for 0% -> 0% of each run, Pallas kernels for 0% -> 0%
where the time goes in v1:
time: 84.1 us; the launch traced here: 83.8 us
  Pallas kernels  74.1 us (88%)
  local copies, waits for them, and re-layouts  8.89 us (11%)
    pallas_call x1, Pallas kernels, layer(): pl.pallas_call(kernel, out_shape=jax.ShapeDtypeStruct((ROWS, FEAT), BF16)...  74.1 us
    unnamed x19, local copies, waits for them, and re-layouts  8.89 us

profile of v1, /device:TPU:16, one launch (start us, length us, event | category | flops | bytes accessed | tf_op | source)
XLA Modules:
  0.0 83.8 jit_solution(14831782412834891033)
XLA Ops:
  0.0 0.0 copy-start.6
  0.7 1.1 %copy.12.queries = bf16[1,128,576]{2,1,0:T(8,128)(2,1)S(1)} copy(bf16[1,128,576]{1,2,0:T(8,128)(2,1)} %param.11) | data formatting | bytes 294912 | tf_op args[0]
  1.8 1.5 %copy.14.out_weight = bf16[1024,448]{1,0:T(8,128)(2,1)S(1)} copy(bf16[1024,448]{0,1:T(8,128)(2,1)} %param.16) | data formatting | bytes 1835008 | tf_op args[5]
  3.3 0.0 copy-done.6
  3.3 0.8 copy.15.down_weight
  4.1 0.0 copy-start
  4.1 0.0 copy-start.3
  4.1 0.0 copy-start.4
  4.1 0.0 copy-start.5
  4.1 2.5 %copy.13.cache = bf16[1,1024,576]{2,1,0:T(8,128)(2,1)} copy(bf16[1,1024,576]{1,2,0:T(8,128)(2,1)} %param.13) | data formatting | bytes 2359296 | tf_op args[2]
  6.6 0.0 copy-done
  6.6 0.0 copy-done.3
  6.6 0.0 copy-done.4
  6.6 0.0 copy-done.5
  6.7 0.0 copy-start.1
  6.7 1.2 %copy-done.1 = bf16[448,1152]{1,0:T(8,128)(2,1)S(1)} copy-done((bf16[448,1152]{1,0:T(8,128)(2,1)S(1)}, bf16[448,1152]{1,0:T(8,128)(2,1)}, u32[]{:S(2)}) %copy-start.1) | copy-done | bytes 1032216
  7.9 0.0 copy-start.2
  7.9 1.2 %copy-done.2 = bf16[448,1152]{1,0:T(8,128)(2,1)S(1)} copy-done((bf16[448,1152]{1,0:T(8,128)(2,1)S(1)}, bf16[448,1152]{1,0:T(8,128)(2,1)}, u32[]{:S(2)}) %copy-start.2) | copy-done | bytes 1032216
  9.1 74.1 %shard_map.109 = bf16[16,448]{1,0:T(8,128)(2,1)S(1)} custom-call(bf16[1,128,576]{2,1,0:T(8,128)(2,1)S(1)} %copy.12.queries, bf16[1,576]{1,0:T(2,128)(2,1)S(1)} %copy-done.4, bf16[1,1024,576]{2,1,0:T(8,128)(2,1)} %copy.13.cache, s32[1]{0:T(128)S(6)} %copy.17.length, bf16[8,512,128]{2,1,0:T(8,128)(2,1)S(1)} %copy-done, bf16[1024,448]{1,0:T(8,128)(2,1)S(1)} %copy.14.out_weight, ...), custom_call_target="tpu_custom_call" | custom-call | tf_op jit(solution)/shard_map/pallas_call | solution.py:419
  83.2 0.6 copy.18
Async XLA Ops:
  0.0 3.3 %copy-start.6 = (bf16[1152,448]{0,1:T(8,128)(2,1)S(1)}, bf16[1152,448]{0,1:T(8,128)(2,1)}, u32[]{:S(2)}) copy-start(bf16[1152,448]{0,1:T(8,128)(2,1)} %param.21) | copy-start | bytes 3096580
  4.1 2.5 %copy-start = (bf16[8,512,128]{2,1,0:T(8,128)(2,1)S(1)}, bf16[8,512,128]{2,1,0:T(8,128)(2,1)}, u32[]{:S(2)}) copy-start(bf16[8,512,128]{2,1,0:T(8,128)(2,1)} %value_up.1) | copy-start | bytes 3145732
  4.1 2.5 %copy-start.3 = (bf16[16,448]{1,0:T(8,128)(2,1)S(1)}, bf16[16,448]{1,0:T(8,128)(2,1)}, u32[]{:S(2)}) copy-start(bf16[16,448]{1,0:T(8,128)(2,1)} %residual.1) | copy-start | bytes 43012
  4.1 2.5 %copy-start.4 = (bf16[1,576]{1,0:T(2,128)(2,1)S(1)}, bf16[1,576]{1,0:T(2,128)(2,1)}, u32[]{:S(2)}) copy-start(bf16[1,576]{1,0:T(2,128)(2,1)} %fresh.1) | copy-start | bytes 3460
  4.1 2.5 %copy-start.5 = (f32[448]{0:T(512)S(1)}, f32[448]{0:T(512)}, u32[]{:S(2)}) copy-start(f32[448]{0:T(512)} %param.18) | copy-start | bytes 5380
  6.7 1.2 %copy-start.1 = (bf16[448,1152]{1,0:T(8,128)(2,1)S(1)}, bf16[448,1152]{1,0:T(8,128)(2,1)}, u32[]{:S(2)}) copy-start(bf16[448,1152]{1,0:T(8,128)(2,1)} %gate_weight.1) | copy-start | bytes 3096580
  7.9 1.2 %copy-start.2 = (bf16[448,1152]{1,0:T(8,128)(2,1)S(1)}, bf16[448,1152]{1,0:T(8,128)(2,1)}, u32[]{:S(2)}) copy-start(bf16[448,1152]{1,0:T(8,128)(2,1)} %up_weight.1) | copy-start | bytes 3096580

commit v2 on v0

v2 whole, which is shorter than its diff:
```python
import jax
import jax.numpy as jnp
from jax import lax
from jax.experimental import pallas as pl
from jax.experimental.pallas import tpu as pltpu
from jax.sharding import PartitionSpec as P

D = 7168
HEADS = 128
LATENT = 512
KEY = 576
CACHE = 1024
SCALE = (128 + 64) ** (-0.5)
PLANE = 16
CHIPS = 8
ROWS = 16
OWN_HEADS = 8
VALUES = 1024
FEAT = 448
PAD = 512
UNITS = 1152
WIDE = 2 * UNITS + 128
F32 = jnp.float32
BF16 = jnp.bfloat16
MESH = pl.DeviceIdType.MESH
SEND_ORDER = (4, 3, 5, 2, 6, 1, 7)
GROUPS = ((0,), (1, 7), (2, 6), (3, 5, 4))
CUTS = ((0, 1280), (1280, WIDE - 1280))


def by_columns(a, b):
    return lax.dot_general(a, b, (((1,), (1,)), ((), ())), preferred_element_type=F32)


def kernel(
    queries,
    fresh,
    cache,
    length,
    value_up,
    out_weight,
    residual,
    gain,
    gate_weight,
    up_weight,
    down_weight,
    out,
    q_v,
    k_v,
    fresh_v,
    residual_v,
    gain_v,
    vu_v,
    ow_v,
    gu_v,
    dw_v,
    head_out,
    head_in,
    val,
    o_out,
    o_in,
    x_out,
    x_in,
    part,
    sum_out,
    sum_in,
    hid,
    d_out,
    d_in,
    load_sem,
    swap_send,
    swap_recv,
    head_sem,
    val_sem,
    o_sem,
    x_sem,
    sum_send,
    sum_recv,
    hid_sem,
    d_sem,
):
    dp, tp = lax.axis_index("dp"), lax.axis_index("tp")
    z, core = lax.div(dp, 2), lax.rem(dp, 2)
    way = 1 - 2 * core
    tp_chip, tp_core = lax.div(tp, 2), lax.rem(tp, 2)
    owns = core == tp_core
    sibling = (dp + way, tp)

    def chip(steps):
        return lax.rem(z + way * steps + 2 * CHIPS, CHIPS)

    def along(steps):
        return (2 * chip(steps) + core, tp)

    def column(steps):
        return lax.rem(tp + steps, PLANE)

    def push(src, dst, send_sem, recv_sem, device):
        copy = pltpu.make_async_remote_copy(src, dst, send_sem, recv_sem, device, MESH)
        copy.start()
        return copy

    def landed(ref, sem):
        pltpu.make_async_remote_copy(ref, ref, sem, sem, sibling, MESH).wait_recv()

    def left(ref, sem):
        pltpu.make_async_remote_copy(ref, ref, sem, sem, sibling, MESH).wait_send()

    def others(ref, sem, wait):
        @pl.when(owns)
        def _():
            wait(ref.at[pl.ds(0, PLANE - 1)], sem)

        @pl.when(jnp.logical_not(owns))
        def _():
            wait(ref, sem)

    def load(src, dst, i):
        copy = pltpu.make_async_copy(src, dst, load_sem.at[i])
        copy.start()
        return copy

    load_q = load(queries.at[0], q_v, 0)
    load_k = load(cache.at[0], k_v, 1)
    load_small = [load(fresh, fresh_v, 2), load(residual, residual_v, 3), load(gain, gain_v, 4)]

    barrier = pltpu.get_barrier_semaphore()
    for i in range(1, PLANE):
        pl.semaphore_signal(barrier, inc=1, device_id=(dp, column(i)), device_id_type=MESH)
    for i in range(PLANE):
        pl.semaphore_signal(
            barrier, inc=1, device_id=(dp + way, column(i)), device_id_type=MESH
        )
    for i in range(1, CHIPS):
        pl.semaphore_signal(barrier, inc=1, device_id=along(i), device_id_type=MESH)

    gu_v[FEAT:PAD, :] = jnp.zeros((PAD - FEAT, WIDE), BF16)
    gu_v[PAD + FEAT :, :] = jnp.zeros((PAD - FEAT, WIDE), BF16)
    gu_v[:, 2 * UNITS :] = jnp.zeros((2 * PAD, WIDE - 2 * UNITS), BF16)
    row = lax.broadcasted_iota(jnp.int32, (16, 128), 0)
    ones = jnp.where(row < 2, 1.0, 0.0).astype(BF16)
    gu_v[FEAT : FEAT + 16, 2 * UNITS :] = ones
    gu_v[PAD + FEAT : PAD + FEAT + 16, 2 * UNITS :] = ones

    load_q.wait()
    load_k.wait()
    for h in range(OWN_HEADS):
        load(value_up.at[h], vu_v.at[:, pl.ds(128 * h, 128)], 5)
    mine = pl.ds(pl.multiple_of(core * PAD, PAD), FEAT)
    weights = [
        (out_weight, ow_v.at[core]),
        (gate_weight, gu_v.at[mine, pl.ds(0, UNITS)]),
        (up_weight, gu_v.at[mine, pl.ds(UNITS, UNITS)]),
        (down_weight, dw_v.at[core]),
    ]
    load_w = [load(src, dst, 6 + i) for i, (src, dst) in enumerate(weights)]
    q = q_v[...].T
    scores = jnp.dot(q, k_v[...], preferred_element_type=F32)
    for copy in load_small:
        copy.wait()
    position = lax.broadcasted_iota(jnp.int32, (HEADS, CACHE), 1)
    scores = jnp.where(position < length[0], scores * SCALE, -1e30)
    new = fresh_v[...].astype(F32)
    own = jnp.sum(q.astype(F32) * new, axis=1, keepdims=True) * SCALE
    top = jnp.maximum(own, jnp.max(scores, axis=1, keepdims=True))
    weight = jnp.exp(scores - top)
    own_weight = jnp.exp(own - top)
    total = jnp.sum(weight, axis=1, keepdims=True) + own_weight
    summed = by_columns(weight.astype(BF16), k_v[:LATENT, :])
    latent = ((summed + own_weight * new[:, :LATENT]) / total).reshape(PLANE, OWN_HEADS, LATENT)
    half = LATENT // 2
    head_out[...] = jnp.concatenate([latent[:, :, :half], latent[:, :, half:]], axis=1).astype(BF16)

    pl.semaphore_wait(barrier, 2 * PLANE - 1 + CHIPS - 1)
    for i in range(1, PLANE):
        to = column(i)
        push(head_out.at[to], head_in.at[tp], head_sem.at[0], head_sem.at[1], (dp, to))
    swaps = [
        push(src, dst, swap_send.at[i], swap_recv.at[i], sibling)
        for i, (src, dst) in enumerate(weights)
    ]
    head_in[tp] = head_out[tp]
    pltpu.make_async_copy(vu_v, vu_v, load_sem.at[5]).wait()
    landed(head_in.at[pl.ds(0, PLANE - 1)], head_sem.at[1])

    wide = head_in[...].astype(F32)
    latents = jnp.concatenate([wide[:, :OWN_HEADS], wide[:, OWN_HEADS:]], axis=2)
    latents = latents.reshape(PLANE * OWN_HEADS, LATENT).astype(BF16)
    products = jnp.dot(latents, vu_v[...], preferred_element_type=F32)
    row_head = lax.broadcasted_iota(jnp.int32, products.shape, 0) & (OWN_HEADS - 1)
    column_head = lax.broadcasted_iota(jnp.int32, products.shape, 1) >> 7
    products = jnp.where(row_head == column_head, products, 0.0).astype(BF16)
    to_row = lax.broadcasted_iota(jnp.int32, (ROWS, PLANE * OWN_HEADS), 0)
    from_row = lax.broadcasted_iota(jnp.int32, (ROWS, PLANE * OWN_HEADS), 1) >> 3
    pick = jnp.where(to_row == from_row, 1.0, 0.0).astype(BF16)
    val[z] = jnp.dot(pick, products, preferred_element_type=F32).astype(BF16)

    def gather(buf, sem, use):
        for d in SEND_ORDER:
            group = [d in g for g in GROUPS].index(True)
            push(buf.at[z], buf.at[z], sem.at[0], sem.at[group], along(d))
        for n, group in enumerate(GROUPS):
            if n:
                landed(buf.at[pl.ds(0, len(group))], sem.at[n])
            use([chip(-d) for d in group])

    def gather_end(buf, sem):
        left(buf.at[pl.ds(0, CHIPS - 1)], sem.at[0])

    def project(buf, w, dst_out, dst_in, sem):
        def use(chips):
            rows = jnp.concatenate([buf[c] for c in chips], axis=0) if len(chips) > 1 else buf[chips[0]]
            for to in range(2):
                sums = by_columns(rows, w[to]).astype(BF16)
                for n, c in enumerate(chips):
                    dst_out[2 * c + to, :, :FEAT] = sums[n * ROWS : (n + 1) * ROWS]
            for c in chips:
                owner = 2 * c + core
                there = dst_out.at[2 * c + 1 - core]
                push(there, dst_in.at[tp], sem.at[0], sem.at[1], (dp + way, owner))

                @pl.when(owner != tp)
                def _():
                    push(dst_out.at[owner], dst_in.at[tp], sem.at[0], sem.at[1], (dp, owner))

                @pl.when(owner == tp)
                def _():
                    dst_in[tp] = dst_out[owner]

        return use

    def collect(dst_in, sem):
        others(dst_in, sem.at[1], landed)
        return jnp.sum(dst_in[...].astype(F32), axis=0)

    load_w[0].wait()
    swaps[0].wait_recv()
    gather(val, val_sem, project(val, ow_v, o_out, o_in, o_sem))
    attention = collect(o_in, o_sem)
    stream = residual_v[...].astype(F32) + attention[:, :FEAT]

    squares = jnp.sum(stream * stream, axis=1, keepdims=True)
    high = squares.astype(BF16).astype(F32)
    lane = lax.broadcasted_iota(jnp.int32, (ROWS, PAD - FEAT), 1)
    extra = jnp.where(lane == 0, high, jnp.where(lane == 1, squares - high, 0.0))
    x_out[:, :FEAT] = (stream * gain_v[...]).astype(BF16)
    x_out[:, FEAT:] = extra.astype(BF16)
    slot = 2 * tp_chip + core
    for i in range(1, PLANE):
        push(x_out, x_in.at[slot], x_sem.at[0], x_sem.at[1], (2 * z + tp_core, column(i)))

    @pl.when(jnp.logical_not(owns))
    def _():
        push(x_out, x_in.at[slot], x_sem.at[0], x_sem.at[1], sibling)

    @pl.when(owns)
    def _():
        x_in[slot] = x_out[...]

    for copy in load_w[1:3]:
        copy.wait()
    for copy in swaps[1:3]:
        copy.wait_recv()
    others(x_in, x_sem.at[1], landed)

    def rows_for(steps):
        blocks = [
            jnp.concatenate([x_in[2 * chip(d)], x_in[2 * chip(d) + 1]], axis=1) for d in steps
        ]
        return jnp.concatenate(blocks, axis=0)

    def onward(value, i, n, device, group):
        lo, size = CUTS[n]
        cut = pl.ds(lo, size)
        sum_out[i, :, lo : lo + size] = value.astype(BF16)
        push(
            sum_out.at[i, :, cut],
            sum_in.at[i, :, cut],
            sum_send.at[n],
            sum_recv.at[n, group],
            along(device),
        )

    def came(first, count, n, group):
        lo, size = CUTS[n]
        landed(sum_in.at[pl.ds(first, count), :, pl.ds(lo, size)], sum_recv.at[n, group])
        return [sum_in[first + k, :, lo : lo + size].astype(F32) for k in range(count)]

    far, near = rows_for((4, 3, -3)), rows_for((1, -1, 2, -2, 0))
    for n, (lo, size) in enumerate(CUTS):
        sums = jnp.dot(far, gu_v[:, lo : lo + size], preferred_element_type=F32)
        onward(sums[:ROWS], 0, n, 2, 0)
        onward(sums[ROWS : 2 * ROWS], 1, n, 1, 0)
        onward(sums[2 * ROWS :], 2, n, -1, 1)
    for n, (lo, size) in enumerate(CUTS):
        sums = jnp.dot(near, gu_v[:, lo : lo + size], preferred_element_type=F32)
        onward(sums[:ROWS], 3, n, 1, 2)
        onward(sums[ROWS : 2 * ROWS], 4, n, -1, 2)
        part[:, lo : lo + size] = sums[2 * ROWS :]
    for n, (lo, size) in enumerate(CUTS):
        a, b = came(0, 2, n, 0)
        onward(part[:ROWS, lo : lo + size] + a + b, 5, n, 2, 2)
        (a,) = came(2, 1, n, 1)
        onward(part[ROWS : 2 * ROWS, lo : lo + size] + a, 6, n, -2, 2)
    whole = []
    for n, (lo, size) in enumerate(CUTS):
        a, b, c, d = came(3, 4, n, 2)
        whole.append(part[2 * ROWS :, lo : lo + size] + (a + b) + (c + d))
    whole = jnp.concatenate(whole, axis=1)
    inverse = lax.rsqrt(whole[:, 2 * UNITS : 2 * UNITS + 1] * (1.0 / D) + 1e-06)
    gate = whole[:, :UNITS] * inverse
    up = whole[:, UNITS : 2 * UNITS] * inverse
    hid[z] = (gate / (1.0 + jnp.exp(-gate)) * up).astype(BF16)

    load_w[3].wait()
    swaps[3].wait_recv()
    gather(hid, hid_sem, project(hid, dw_v, d_out, d_in, d_sem))
    lowered = collect(d_in, d_sem)
    out[...] = (stream + lowered[:, :FEAT]).astype(BF16)

    for copy in swaps:
        copy.wait_send()
    left(head_out.at[pl.ds(0, PLANE - 1)], head_sem.at[0])
    gather_end(val, val_sem)
    others(o_out, o_sem.at[0], left)
    others(x_in, x_sem.at[0], left)
    for n, (lo, size) in enumerate(CUTS):
        left(sum_out.at[:, :, pl.ds(lo, size)], sum_send.at[n])
    gather_end(hid, hid_sem)
    others(d_out, d_sem.at[0], left)


def layer(
    queries,
    new_latent,
    latent_cache,
    cached_lengths,
    value_up,
    out_weight,
    residual_in,
    norm_gain,
    gate_weight,
    up_weight,
    down_weight,
):
    anywhere = pl.BlockSpec(memory_space=pl.ANY)
    smem = pl.BlockSpec(memory_space=pltpu.SMEM)
    dma = pltpu.SemaphoreType.DMA
    return pl.pallas_call(
        kernel,
        out_shape=jax.ShapeDtypeStruct((ROWS, FEAT), BF16),
        in_specs=[anywhere] * 3 + [smem] + [anywhere] * 7,
        out_specs=pl.BlockSpec(memory_space=pltpu.VMEM),
        scratch_shapes=[
            pltpu.VMEM((KEY, HEADS), BF16),
            pltpu.VMEM((KEY, CACHE), BF16),
            pltpu.VMEM((1, KEY), BF16),
            pltpu.VMEM((ROWS, FEAT), BF16),
            pltpu.VMEM((1, FEAT), F32),
            pltpu.VMEM((LATENT, VALUES), BF16),
            pltpu.VMEM((2, FEAT, VALUES), BF16),
            pltpu.VMEM((2 * PAD, WIDE), BF16),
            pltpu.VMEM((2, FEAT, UNITS), BF16),
            pltpu.VMEM((PLANE, ROWS, LATENT // 2), BF16),
            pltpu.VMEM((PLANE, ROWS, LATENT // 2), BF16),
            pltpu.VMEM((CHIPS, ROWS, VALUES), BF16),
            pltpu.VMEM((PLANE, ROWS, PAD), BF16),
            pltpu.VMEM((PLANE, ROWS, PAD), BF16),
            pltpu.VMEM((ROWS, PAD), BF16),
            pltpu.VMEM((PLANE, ROWS, PAD), BF16),
            pltpu.VMEM((3 * ROWS, WIDE), F32),
            pltpu.VMEM((7, ROWS, WIDE), BF16),
            pltpu.VMEM((7, ROWS, WIDE), BF16),
            pltpu.VMEM((CHIPS, ROWS, UNITS), BF16),
            pltpu.VMEM((PLANE, ROWS, PAD), BF16),
            pltpu.VMEM((PLANE, ROWS, PAD), BF16),
            dma((10,)),
            dma((4,)),
            dma((4,)),
            dma((2,)),
            dma((len(GROUPS),)),
            dma((2,)),
            dma((2,)),
            dma((len(CUTS),)),
            dma((len(CUTS), 3)),
            dma((len(GROUPS),)),
            dma((2,)),
        ],
        compiler_params=pltpu.CompilerParams(
            collective_id=0, has_side_effects=True, vmem_limit_bytes=60 * 1024 * 1024
        ),
    )(
        queries.transpose(0, 2, 1),
        new_latent,
        latent_cache.transpose(0, 2, 1),
        cached_lengths,
        value_up,
        out_weight.T,
        residual_in,
        norm_gain.reshape(1, FEAT),
        gate_weight,
        up_weight,
        down_weight.T,
    )


def solution(mesh):
    in_specs = (
        P(("dp", "tp"), None, None),
        P(("dp", "tp"), None),
        P(("dp", "tp"), None, None),
        P(("dp", "tp")),
        P("tp", None, None),
        P("tp", "dp"),
        P("tp", "dp"),
        P("dp"),
        P("dp", "tp"),
        P("dp", "tp"),
        P("tp", "dp"),
    )
    return jax.shard_map(
        layer, mesh=mesh, in_specs=in_specs, out_specs=P("tp", "dp"), check_vma=False
    )
```

time: 384 us -> 67 us (0.17)
  waiting for transfers between devices: 267 us -> 0 us
  blocking collectives: 80.5 us -> 0 us
  Pallas kernels: 0 us -> 64.2 us
  matrix products: 14.2 us -> 0 us
  between operations: 13.2 us -> 0.66 us
  other arithmetic: 6.86 us -> 0 us
    reduce_scatter x2 -> x0, waiting for transfers between devices: 151 us -> none  [the longest x1 77.7 us: shards(): lax.psum_scatter(jnp.dot(row_block, down_weight, preferred_element_type=j...]
    psum x1 -> x0, waiting for transfers between devices: 116 us -> none  [shards(): gate_sum, up_sum = lax.psum((gate_sum, up_sum), 'dp')]
    pallas_call x0 -> x1, Pallas kernels: none -> 64.2 us  [layer(): pl.pallas_call(kernel, out_shape=jax.ShapeDtypeStruct((ROWS, FEAT), BF16)...]
    all_gather x2 -> x0, blocking collectives: 43.8 us -> none  [the longest x1 22.4 us: shards(): row_piece = lax.all_gather(normed, 'tp', axis=0, tiled=True)]
    psum x1 -> x0, blocking collectives: 24.1 us -> none  [shards(): square_sum = lax.psum(partial_value, 'dp')]
    dot_general x10 -> x0, matrix products: 14.2 us -> none  [the longest x2 2.96 us: visit(): jnp.einsum('rhc,rkc->rhk', queries, key_block, preferred_element_type=jnp...]
    all_to_all x1 -> x0, blocking collectives: 12.6 us -> none  [shards(): lax.all_to_all(head_latent, 'tp', split_axis=1, concat_axis=0, tiled=True)]
  transfers between devices with their start and end apart: 3 -> 0, of which waited for: 3 -> 0; matrix products, arithmetic and copies ran while one was open for 0% -> 0% of each run, Pallas kernels for 0% -> 0%
where the time goes in v2:
time: 67 us; the launch traced here: 66.2 us
  Pallas kernels  64.2 us (96%)
  local copies, waits for them, and re-layouts  1.32 us (2%)
    pallas_call x1, Pallas kernels, layer(): pl.pallas_call(kernel, out_shape=jax.ShapeDtypeStruct((ROWS, FEAT), BF16)...  64.2 us

profile of v2, /device:TPU:16, one launch (start us, length us, event | category | flops | bytes accessed | tf_op | source)
XLA Modules:
  0.0 66.2 jit_solution(3342916129738428068)
XLA Ops:
  0.7 64.2 %shard_map.109 = bf16[16,448]{1,0:T(8,128)(2,1)} custom-call(bf16[1,576,128]{2,1,0:T(8,128)(2,1)} %bitcast.8, bf16[1,576]{1,0:T(2,128)(2,1)} %fresh.1, bf16[1,576,1024]{2,1,0:T(8,128)(2,1)} %bitcast.5, s32[1]{0:T(128)S(6)} %copy.13.length, bf16[8,512,128]{2,1,0:T(8,128)(2,1)} %value_up.1, bf16[448,1024]{1,0:T(8,128)(2,1)} %bitcast.7, ...), custom_call_target="tpu_custom_call" | custom-call | tf_op jit(solution)/shard_map/pallas_call | solution.py:349
  64.8 1.3 %copy.14 = bf16[16,448]{1,0:T(8,128)(2,1)} copy(bf16[16,448]{1,0:T(8,128)(2,1)} %shard_map.109) | data formatting | bytes 28672

commit v3 on v2

--- a/solution.py
+++ b/solution.py
@@ -23,9 +23,10 @@
 F32 = jnp.float32
 BF16 = jnp.bfloat16
 MESH = pl.DeviceIdType.MESH
-SEND_ORDER = (4, 3, 5, 2, 6, 1, 7)
-GROUPS = ((0,), (1, 7), (2, 6), (3, 5, 4))
-CUTS = ((0, 1280), (1280, WIDE - 1280))
+FAR_FIRST = (10, 6, 9, 11, 14, 5, 7, 13, 15, 2, 8, 1, 3, 4, 12)
+SEND_ORDER = (1, 7, 4, 2, 6, 3, 5)
+GROUPS = ((0,), (1, 7), (2, 6, 4), (3, 5))
+CUTS = ((0, 768), (768, 768), (1536, WIDE - 1536))
 
 
 def by_columns(a, b):
@@ -47,6 +48,7 @@
     out,
     q_v,
     k_v,
+    length_s,
     fresh_v,
     residual_v,
     gain_v,
@@ -84,16 +86,19 @@
     way = 1 - 2 * core
     tp_chip, tp_core = lax.div(tp, 2), lax.rem(tp, 2)
     owns = core == tp_core
+    owns_later = core != tp_core
     sibling = (dp + way, tp)
+    spin = 1 + 2 * lax.rem(tp + lax.div(tp, 4), 2)
 
     def chip(steps):
-        return lax.rem(z + way * steps + 2 * CHIPS, CHIPS)
+        return lax.rem(z + way * steps + 4 * CHIPS, CHIPS)
 
     def along(steps):
         return (2 * chip(steps) + core, tp)
 
     def column(steps):
         return lax.rem(tp + steps, PLANE)
+
 
     def push(src, dst, send_sem, recv_sem, device):
         copy = pltpu.make_async_remote_copy(src, dst, send_sem, recv_sem, device, MESH)
@@ -106,12 +111,12 @@
     def left(ref, sem):
         pltpu.make_async_remote_copy(ref, ref, sem, sem, sibling, MESH).wait_send()
 
-    def others(ref, sem, wait):
-        @pl.when(owns)
+    def others(ref, sem, wait, owned):
+        @pl.when(owned)
         def _():
             wait(ref.at[pl.ds(0, PLANE - 1)], sem)
 
-        @pl.when(jnp.logical_not(owns))
+        @pl.when(jnp.logical_not(owned))
         def _():
             wait(ref, sem)
 
@@ -122,10 +127,15 @@
 
     load_q = load(queries.at[0], q_v, 0)
     load_k = load(cache.at[0], k_v, 1)
-    load_small = [load(fresh, fresh_v, 2), load(residual, residual_v, 3), load(gain, gain_v, 4)]
+    load_small = [
+        load(fresh, fresh_v, 2),
+        load(residual, residual_v, 3),
+        load(gain, gain_v, 4),
+        load(length, length_s, 10),
+    ]
 
     barrier = pltpu.get_barrier_semaphore()
-    for i in range(1, PLANE):
+    for i in FAR_FIRST:
         pl.semaphore_signal(barrier, inc=1, device_id=(dp, column(i)), device_id_type=MESH)
     for i in range(PLANE):
         pl.semaphore_signal(
@@ -159,7 +169,7 @@
     for copy in load_small:
         copy.wait()
     position = lax.broadcasted_iota(jnp.int32, (HEADS, CACHE), 1)
-    scores = jnp.where(position < length[0], scores * SCALE, -1e30)
+    scores = jnp.where(position < length_s[0], scores * SCALE, -1e30)
     new = fresh_v[...].astype(F32)
     own = jnp.sum(q.astype(F32) * new, axis=1, keepdims=True) * SCALE
     top = jnp.maximum(own, jnp.max(scores, axis=1, keepdims=True))
@@ -172,7 +182,7 @@
     head_out[...] = jnp.concatenate([latent[:, :, :half], latent[:, :, half:]], axis=1).astype(BF16)
 
     pl.semaphore_wait(barrier, 2 * PLANE - 1 + CHIPS - 1)
-    for i in range(1, PLANE):
+    for i in FAR_FIRST:
         to = column(i)
         push(head_out.at[to], head_in.at[tp], head_sem.at[0], head_sem.at[1], (dp, to))
     swaps = [
@@ -198,16 +208,16 @@
     def gather(buf, sem, use):
         for d in SEND_ORDER:
             group = [d in g for g in GROUPS].index(True)
-            push(buf.at[z], buf.at[z], sem.at[0], sem.at[group], along(d))
+            push(buf.at[z], buf.at[z], sem.at[0], sem.at[group], along(spin * d))
         for n, group in enumerate(GROUPS):
             if n:
                 landed(buf.at[pl.ds(0, len(group))], sem.at[n])
-            use([chip(-d) for d in group])
+            use([chip(-spin * d) for d in group])
 
     def gather_end(buf, sem):
         left(buf.at[pl.ds(0, CHIPS - 1)], sem.at[0])
 
-    def project(buf, w, dst_out, dst_in, sem):
+    def project(buf, w, dst_out, dst_in, sem, parity):
         def use(chips):
             rows = jnp.concatenate([buf[c] for c in chips], axis=0) if len(chips) > 1 else buf[chips[0]]
             for to in range(2):
@@ -215,28 +225,29 @@
                 for n, c in enumerate(chips):
                     dst_out[2 * c + to, :, :FEAT] = sums[n * ROWS : (n + 1) * ROWS]
             for c in chips:
-                owner = 2 * c + core
+                owner = 2 * c + parity
+                here = dst_out.at[2 * c + core]
                 there = dst_out.at[2 * c + 1 - core]
                 push(there, dst_in.at[tp], sem.at[0], sem.at[1], (dp + way, owner))
 
                 @pl.when(owner != tp)
                 def _():
-                    push(dst_out.at[owner], dst_in.at[tp], sem.at[0], sem.at[1], (dp, owner))
+                    push(here, dst_in.at[tp], sem.at[0], sem.at[1], (dp, owner))
 
                 @pl.when(owner == tp)
                 def _():
-                    dst_in[tp] = dst_out[owner]
+                    dst_in[tp] = here[...]
 
         return use
 
-    def collect(dst_in, sem):
-        others(dst_in, sem.at[1], landed)
+    def collect(dst_in, sem, owned):
+        others(dst_in, sem.at[1], landed, owned)
         return jnp.sum(dst_in[...].astype(F32), axis=0)
 
     load_w[0].wait()
     swaps[0].wait_recv()
-    gather(val, val_sem, project(val, ow_v, o_out, o_in, o_sem))
-    attention = collect(o_in, o_sem)
+    gather(val, val_sem, project(val, ow_v, o_out, o_in, o_sem, core))
+    attention = collect(o_in, o_sem, owns)
     stream = residual_v[...].astype(F32) + attention[:, :FEAT]
 
     squares = jnp.sum(stream * stream, axis=1, keepdims=True)
@@ -246,14 +257,14 @@
     x_out[:, :FEAT] = (stream * gain_v[...]).astype(BF16)
     x_out[:, FEAT:] = extra.astype(BF16)
     slot = 2 * tp_chip + core
-    for i in range(1, PLANE):
-        push(x_out, x_in.at[slot], x_sem.at[0], x_sem.at[1], (2 * z + tp_core, column(i)))
-
-    @pl.when(jnp.logical_not(owns))
+    for i in FAR_FIRST:
+        push(x_out, x_in.at[slot], x_sem.at[0], x_sem.at[1], (2 * z + 1 - tp_core, column(i)))
+
+    @pl.when(owns)
     def _():
         push(x_out, x_in.at[slot], x_sem.at[0], x_sem.at[1], sibling)
 
-    @pl.when(owns)
+    @pl.when(owns_later)
     def _():
         x_in[slot] = x_out[...]
 
@@ -261,7 +272,7 @@
         copy.wait()
     for copy in swaps[1:3]:
         copy.wait_recv()
-    others(x_in, x_sem.at[1], landed)
+    others(x_in, x_sem.at[1], landed, owns_later)
 
     def rows_for(steps):
         blocks = [
@@ -314,20 +325,20 @@
 
     load_w[3].wait()
     swaps[3].wait_recv()
-    gather(hid, hid_sem, project(hid, dw_v, d_out, d_in, d_sem))
-    lowered = collect(d_in, d_sem)
+    gather(hid, hid_sem, project(hid, dw_v, d_out, d_in, d_sem, 1 - core))
+    lowered = collect(d_in, d_sem, owns_later)
     out[...] = (stream + lowered[:, :FEAT]).astype(BF16)
 
     for copy in swaps:
         copy.wait_send()
     left(head_out.at[pl.ds(0, PLANE - 1)], head_sem.at[0])
     gather_end(val, val_sem)
-    others(o_out, o_sem.at[0], left)
-    others(x_in, x_sem.at[0], left)
+    others(o_out, o_sem.at[0], left, owns)
+    others(x_in, x_sem.at[0], left, owns_later)
     for n, (lo, size) in enumerate(CUTS):
         left(sum_out.at[:, :, pl.ds(lo, size)], sum_send.at[n])
     gather_end(hid, hid_sem)
-    others(d_out, d_sem.at[0], left)
+    others(d_out, d_sem.at[0], left, owns_later)
 
 
 def layer(
@@ -344,16 +355,16 @@
     down_weight,
 ):
     anywhere = pl.BlockSpec(memory_space=pl.ANY)
-    smem = pl.BlockSpec(memory_space=pltpu.SMEM)
     dma = pltpu.SemaphoreType.DMA
     return pl.pallas_call(
         kernel,
         out_shape=jax.ShapeDtypeStruct((ROWS, FEAT), BF16),
-        in_specs=[anywhere] * 3 + [smem] + [anywhere] * 7,
+        in_specs=[anywhere] * 11,
         out_specs=pl.BlockSpec(memory_space=pltpu.VMEM),
         scratch_shapes=[
             pltpu.VMEM((KEY, HEADS), BF16),
             pltpu.VMEM((KEY, CACHE), BF16),
+            pltpu.SMEM((1,), jnp.int32),
             pltpu.VMEM((1, KEY), BF16),
             pltpu.VMEM((ROWS, FEAT), BF16),
             pltpu.VMEM((1, FEAT), F32),
@@ -374,7 +385,7 @@
             pltpu.VMEM((CHIPS, ROWS, UNITS), BF16),
             pltpu.VMEM((PLANE, ROWS, PAD), BF16),
             pltpu.VMEM((PLANE, ROWS, PAD), BF16),
-            dma((10,)),
+            dma((11,)),
             dma((4,)),
             dma((4,)),
             dma((2,)),

time: 67 us -> 62.7 us (0.936)
  the two profiles are of different devices: /device:TPU:16 before, /device:TPU:6 now
where the time goes in v3:
time: 62.7 us; the launch traced here: 62.5 us
  Pallas kernels  60.5 us (96%)
  local copies, waits for them, and re-layouts  1.32 us (2%)
  between operations  0.66 us (1%)
    pallas_call x1, Pallas kernels, layer(): pl.pallas_call(kernel, out_shape=jax.ShapeDtypeStruct((ROWS, FEAT), BF16)...  60.5 us
    unnamed x1, local copies, waits for them, and re-layouts  1.32 us

profile of v3, /device:TPU:6, one launch (start us, length us, event | category | flops | bytes accessed | tf_op | source)
XLA Modules:
  0.0 62.5 jit_solution(4087113796727559505)
XLA Ops:
  0.7 60.5 %shard_map.109 = bf16[16,448]{1,0:T(8,128)(2,1)} custom-call(bf16[1,576,128]{2,1,0:T(8,128)(2,1)} %bitcast.8, bf16[1,576]{1,0:T(2,128)(2,1)} %fresh.1, bf16[1,576,1024]{2,1,0:T(8,128)(2,1)} %bitcast.5, s32[1]{0:T(128)S(6)} %copy.13.length, bf16[8,512,128]{2,1,0:T(8,128)(2,1)} %value_up.1, bf16[448,1024]{1,0:T(8,128)(2,1)} %bitcast.7, ...), custom_call_target="tpu_custom_call" | custom-call | tf_op jit(solution)/shard_map/pallas_call | solution.py:359
  61.2 1.3 %copy.14 = bf16[16,448]{1,0:T(8,128)(2,1)} copy(bf16[16,448]{1,0:T(8,128)(2,1)} %shard_map.109) | data formatting | bytes 28672

commit v4 on v3

--- a/solution.py
+++ b/solution.py
@@ -24,8 +24,8 @@
 BF16 = jnp.bfloat16
 MESH = pl.DeviceIdType.MESH
 FAR_FIRST = (10, 6, 9, 11, 14, 5, 7, 13, 15, 2, 8, 1, 3, 4, 12)
-SEND_ORDER = (1, 7, 4, 2, 6, 3, 5)
-GROUPS = ((0,), (1, 7), (2, 6, 4), (3, 5))
+VAL_PLAN = ((1, 7, 2, 6, 3, 5, 4), {}, ((0,), (1, 7), (2, 6), (3, 5, 4)))
+HID_PLAN = ((2, 6, 1, 7), {2: (2, 1), 6: (-1,)}, ((0,), (2, 6), (1, 7), (3, 5, 4)))
 CUTS = ((0, 768), (768, 768), (1536, WIDE - 1536))
 
 
@@ -88,10 +88,9 @@
     owns = core == tp_core
     owns_later = core != tp_core
     sibling = (dp + way, tp)
-    spin = 1 + 2 * lax.rem(tp + lax.div(tp, 4), 2)
 
     def chip(steps):
-        return lax.rem(z + way * steps + 4 * CHIPS, CHIPS)
+        return lax.rem(z + way * steps + 2 * CHIPS, CHIPS)
 
     def along(steps):
         return (2 * chip(steps) + core, tp)
@@ -205,14 +204,20 @@
     pick = jnp.where(to_row == from_row, 1.0, 0.0).astype(BF16)
     val[z] = jnp.dot(pick, products, preferred_element_type=F32).astype(BF16)
 
-    def gather(buf, sem, use):
-        for d in SEND_ORDER:
-            group = [d in g for g in GROUPS].index(True)
-            push(buf.at[z], buf.at[z], sem.at[0], sem.at[group], along(spin * d))
-        for n, group in enumerate(GROUPS):
+    def gather(buf, sem, use, order, relays, groups):
+        def group_of(d):
+            return [d % CHIPS in g for g in groups].index(True)
+
+        for d in order:
+            push(buf.at[z], buf.at[z], sem.at[0], sem.at[group_of(d)], along(d))
+        for n, group in enumerate(groups):
             if n:
                 landed(buf.at[pl.ds(0, len(group))], sem.at[n])
-            use([chip(-spin * d) for d in group])
+            for d in group:
+                for step in relays.get(d, ()):
+                    block = buf.at[chip(-d)]
+                    push(block, block, sem.at[0], sem.at[group_of(d + step)], along(step))
+            use([chip(-d) for d in group])
 
     def gather_end(buf, sem):
         left(buf.at[pl.ds(0, CHIPS - 1)], sem.at[0])
@@ -246,7 +251,7 @@
 
     load_w[0].wait()
     swaps[0].wait_recv()
-    gather(val, val_sem, project(val, ow_v, o_out, o_in, o_sem, core))
+    gather(val, val_sem, project(val, ow_v, o_out, o_in, o_sem, core), *VAL_PLAN)
     attention = collect(o_in, o_sem, owns)
     stream = residual_v[...].astype(F32) + attention[:, :FEAT]
 
@@ -325,7 +330,7 @@
 
     load_w[3].wait()
     swaps[3].wait_recv()
-    gather(hid, hid_sem, project(hid, dw_v, d_out, d_in, d_sem, 1 - core))
+    gather(hid, hid_sem, project(hid, dw_v, d_out, d_in, d_sem, 1 - core), *HID_PLAN)
     lowered = collect(d_in, d_sem, owns_later)
     out[...] = (stream + lowered[:, :FEAT]).astype(BF16)
 
@@ -389,12 +394,12 @@
             dma((4,)),
             dma((4,)),
             dma((2,)),
-            dma((len(GROUPS),)),
+            dma((4,)),
             dma((2,)),
             dma((2,)),
             dma((len(CUTS),)),
             dma((len(CUTS), 3)),
-            dma((len(GROUPS),)),
+            dma((4,)),
             dma((2,)),
         ],
         compiler_params=pltpu.CompilerParams(

time: 62.7 us -> 61 us (0.973)
  the two profiles are of different devices: /device:TPU:6 before, /device:TPU:16 now
where the time goes in v4:
time: 61 us; the launch traced here: 60.4 us
  Pallas kernels  58.4 us (96%)
  local copies, waits for them, and re-layouts  1.32 us (2%)
  between operations  0.66 us (1%)
    pallas_call x1, Pallas kernels, layer(): pl.pallas_call(kernel, out_shape=jax.ShapeDtypeStruct((ROWS, FEAT), BF16)...  58.4 us
    unnamed x1, local copies, waits for them, and re-layouts  1.32 us

profile of v4, /device:TPU:16, one launch (start us, length us, event | category | flops | bytes accessed | tf_op | source)
XLA Modules:
  0.0 60.4 jit_solution(3393018702419319198)
XLA Ops:
  0.7 58.4 %shard_map.109 = bf16[16,448]{1,0:T(8,128)(2,1)} custom-call(bf16[1,576,128]{2,1,0:T(8,128)(2,1)} %bitcast.8, bf16[1,576]{1,0:T(2,128)(2,1)} %fresh.1, bf16[1,576,1024]{2,1,0:T(8,128)(2,1)} %bitcast.5, s32[1]{0:T(128)S(6)} %copy.13.length, bf16[8,512,128]{2,1,0:T(8,128)(2,1)} %value_up.1, bf16[448,1024]{1,0:T(8,128)(2,1)} %bitcast.7, ...), custom_call_target="tpu_custom_call" | custom-call | tf_op jit(solution)/shard_map/pallas_call | solution.py:364
  59.1 1.3 %copy.14 = bf16[16,448]{1,0:T(8,128)(2,1)} copy(bf16[16,448]{1,0:T(8,128)(2,1)} %shard_map.109) | data formatting | bytes 28672

commit v5 on v4

--- a/solution.py
+++ b/solution.py
@@ -26,7 +26,7 @@
 FAR_FIRST = (10, 6, 9, 11, 14, 5, 7, 13, 15, 2, 8, 1, 3, 4, 12)
 VAL_PLAN = ((1, 7, 2, 6, 3, 5, 4), {}, ((0,), (1, 7), (2, 6), (3, 5, 4)))
 HID_PLAN = ((2, 6, 1, 7), {2: (2, 1), 6: (-1,)}, ((0,), (2, 6), (1, 7), (3, 5, 4)))
-CUTS = ((0, 768), (768, 768), (1536, WIDE - 1536))
+CUTS = ((0, 640), (640, 640), (1280, 640), (1920, WIDE - 1920))
 
 
 def by_columns(a, b):
@@ -229,19 +229,18 @@
                 sums = by_columns(rows, w[to]).astype(BF16)
                 for n, c in enumerate(chips):
                     dst_out[2 * c + to, :, :FEAT] = sums[n * ROWS : (n + 1) * ROWS]
-            for c in chips:
-                owner = 2 * c + parity
-                here = dst_out.at[2 * c + core]
-                there = dst_out.at[2 * c + 1 - core]
-                push(there, dst_in.at[tp], sem.at[0], sem.at[1], (dp + way, owner))
-
-                @pl.when(owner != tp)
-                def _():
-                    push(here, dst_in.at[tp], sem.at[0], sem.at[1], (dp, owner))
-
-                @pl.when(owner == tp)
-                def _():
-                    dst_in[tp] = here[...]
+                for c in chips:
+                    block = dst_out.at[2 * c + to]
+                    owner = 2 * c + parity
+                    mine = jnp.logical_and(core == to, owner == tp)
+
+                    @pl.when(jnp.logical_not(mine))
+                    def _():
+                        push(block, dst_in.at[tp], sem.at[0], sem.at[1], (2 * z + to, owner))
+
+                    @pl.when(mine)
+                    def _():
+                        dst_in[tp] = block[...]
 
         return use
 

time: 61 us -> 60.8 us (level)
  no operation moved by 1% of the time
where the time goes in v5:
time: 60.8 us; the launch traced here: 59.9 us
  Pallas kernels  57.9 us (95%)
  local copies, waits for them, and re-layouts  1.32 us (2%)
  between operations  0.66 us (1%)
    pallas_call x1, Pallas kernels, layer(): pl.pallas_call(kernel, out_shape=jax.ShapeDtypeStruct((ROWS, FEAT), BF16)...  57.9 us
    unnamed x1, local copies, waits for them, and re-layouts  1.32 us

profile of v5, /device:TPU:16, one launch (start us, length us, event | category | flops | bytes accessed | tf_op | source)
XLA Modules:
  0.0 59.9 jit_solution(51714069113138230)
XLA Ops:
  0.7 57.9 %shard_map.109 = bf16[16,448]{1,0:T(8,128)(2,1)} custom-call(bf16[1,576,128]{2,1,0:T(8,128)(2,1)} %bitcast.8, bf16[1,576]{1,0:T(2,128)(2,1)} %fresh.1, bf16[1,576,1024]{2,1,0:T(8,128)(2,1)} %bitcast.5, s32[1]{0:T(128)S(6)} %copy.13.length, bf16[8,512,128]{2,1,0:T(8,128)(2,1)} %value_up.1, bf16[448,1024]{1,0:T(8,128)(2,1)} %bitcast.7, ...), custom_call_target="tpu_custom_call" | custom-call | tf_op jit(solution)/shard_map/pallas_call | solution.py:363
  58.6 1.3 %copy.14 = bf16[16,448]{1,0:T(8,128)(2,1)} copy(bf16[16,448]{1,0:T(8,128)(2,1)} %shard_map.109) | data formatting | bytes 28672
